TPU v7x, 256 devices: a whole 4x4x8 slice. The times are simulated.
256 devices in a mesh: row: 8 (over x_hi, y), col: 32 (over z, x_lo, core).
Axes of the slice: x: 4 (x_hi: 2, x_lo: 2; x = x_hi * 2 + x_lo), y: 4, z: 8, core: 2. Of those that a mesh axis runs over, the one named last changes fastest.
Arguments:
- query_grads: bfloat16 [2, 8192, 28672], P(None, 'row', 'col'), may hold values from -6 to 6
- basis_in: bfloat16 [8192, 1024], P('row', 'col'), may hold values from -0.1875 to 0.1875
- basis_out: bfloat16 [28672, 1024], P('col', 'row'), may hold values from -0.03125 to 0.03125
- eig_in: float32 [1024], P('row'), may hold values from 0.1 to 1
- eig_out: float32 [1024], P('col'), may hold values from 0.1 to 1
- damping: float32 [1], replicated, may hold values from 0.02 to 0.2
Outputs:
- preconditioned: bfloat16 [2, 8192, 28672], P(None, 'row', 'col')
All inputs are finite; a program needn't handle non-finite values.
Results may differ from a plain program's by a relative error of at most 0.023.
Values may be sent and summed in bfloat16 or wider, within the bound.
A program may use at most 128 MiB of HBM per device.

v0:
```python
import jax
import jax.numpy as jnp
from jax import lax
from jax.sharding import PartitionSpec as P


def body(query_grads, basis_in, basis_out, eig_in, eig_out, damping):
    in_rows = lax.all_gather(basis_in, "col", axis=1, tiled=True)
    out_rows = lax.all_gather(basis_out, "row", axis=1, tiled=True)
    block = in_rows
    partial_left = lax.psum_scatter(
        jnp.einsum("qdf,da->aqf", query_grads, block, preferred_element_type=jnp.float32).astype(
            jnp.bfloat16
        ),
        "row",
        scatter_dimension=0,
        tiled=True,
    ).astype(jnp.float32)
    block = out_rows.astype(jnp.float32)
    rotated = lax.psum_scatter(
        jnp.einsum("aqf,fs->sqa", partial_left, block, precision=lax.Precision.HIGHEST),
        "col",
        scatter_dimension=0,
        tiled=True,
    )
    denom = eig_out[:, None, None] * eig_in[None, None, :] + damping[0]
    scaled = (rotated / denom).astype(jnp.bfloat16)
    scaled_all = lax.all_gather(scaled, "col", axis=0, tiled=True)
    back_half = jnp.einsum(
        "sqa,fs->aqf", scaled_all, out_rows, preferred_element_type=jnp.float32
    ).astype(jnp.bfloat16)
    block = in_rows
    result = jnp.einsum(
        "da,aqf->qdf",
        block,
        lax.all_gather(back_half, "row", axis=0, tiled=True),
        preferred_element_type=jnp.float32,
    )
    return result.astype(jnp.bfloat16)


def solution(mesh):
    return jax.shard_map(
        body,
        mesh=mesh,
        in_specs=(P(None, "row", "col"), P("row", "col"), P("col", "row"), P("row"), P("col"), P()),
        out_specs=P(None, "row", "col"),
        check_vma=False,
    )
```

profile of v0, /device:TPU:1, one launch (start us, length us, event | category | flops | bytes accessed | tf_op | source)
XLA Modules:
  0.0 616.2 jit_solution(1946487602861871391)
XLA Ops:
  6.5 0.0 all-gather.4.cloned.1.call-start
  6.5 0.7 all-gather.4.cloned.1.call-update
  7.3 0.0 all-reduce.5.cloned.1.call-start
  7.3 70.8 %all-gather.4.cloned.1.call-done = bf16[1024,1024]{0,1:T(8,128)(2,1)} async-done(((bf16[1024,32]{0,1:T(8,128)(2,1)}), bf16[1024,1024]{0,1:T(8,128)(2,1)}) %all-gather.4.cloned.1.call-update) | async-done | bytes 2097168 | tf_op jit(solution)/shard_map/all_gather | solution.py:8
  78.1 6.6 %fusion.1 = bf16[1024,2,896]{2,0,1:T(8,128)(2,1)S(1)} fusion(bf16[2,1024,896]{2,1,0:T(8,128)(2,1)} %param.6, bf16[1024,1024]{0,1:T(8,128)(2,1)} %all-gather.4.cloned.1.call-done), kind=kOutput, calls=%fused_computation.3 | convolution fusion | flops 3758096384 | bytes 9437184 | tf_op jit(solution)/shard_map/qdf,da->aqf/dot_general | solution.py:12
  84.8 5.6 copy.18
  90.4 0.0 copy-start.4
  90.4 0.0 all-reduce.5.cloned.1.call-update
  90.4 0.0 all-gather.6.cloned.1.call-start
  90.4 0.7 all-gather.6.cloned.1.call-update
  91.1 0.0 all-reduce.7.cloned.1.call-start
  91.2 0.0 copy-done.4
  91.2 0.6 dynamic-slice
  92.4 0.0 copy-start.3
  92.4 0.0 copy-start.1
  92.4 0.0 copy-start.2
  92.5 103.6 %all-reduce.5.cloned.1.call-done = bf16[1024,2,896]{2,1,0:T(2,128)(2,1)} async-done(((bf16[1024,2,896]{2,1,0:T(2,128)(2,1)}), bf16[1024,2,896]{2,1,0:T(2,128)(2,1)}) %all-reduce.5.cloned.1.call-update) | async-done | bytes 3670032
  196.1 1.3 constant_dynamic-slice_fusion
  197.4 59.8 %all-gather.6.cloned.1.call-done = bf16[896,1024]{1,0:T(8,128)(2,1)} async-done(((bf16[896,128]{1,0:T(8,128)(2,1)}), bf16[896,1024]{1,0:T(8,128)(2,1)}) %all-gather.6.cloned.1.call-update) | async-done | bytes 1835024 | tf_op jit(solution)/shard_map/all_gather | solution.py:9
  257.2 0.0 copy-start
  257.2 2.3 fusion.5
  259.5 1.3 copy.11
  260.8 0.0 all-reduce.7.cloned.1.call-update
  260.9 0.0 all-gather.8.cloned.1.call-start
  260.9 0.0 copy-done.3
  260.9 0.6 dynamic-slice.2
  262.8 0.0 copy-done.1
  262.8 0.0 copy-done.2
  262.8 0.1 multiply_add_fusion
  262.9 223.6 %all-reduce.7.cloned.1.call-done = f32[1024,2,128]{2,1,0:T(2,128)} async-done(((f32[1024,2,128]{2,1,0:T(2,128)}), f32[1024,2,128]{2,1,0:T(2,128)}) %all-reduce.7.cloned.1.call-update) | async-done | bytes 1048592
  486.4 0.8 fusion.15
  487.2 32.7 %all_gather.14 = bf16[1024,2,128]{2,1,0:T(2,128)(2,1)S(1)} all-gather(bf16[32,2,128]{2,1,0:T(2,128)(2,1)S(1)} %fusion.15), channel_id=1, replica_groups=mesh['row'=8,'col'=32] {'col'}, dimensions={0}, use_global_device_ids=true | all-gather | bytes 540672 | tf_op jit(solution)/shard_map/all_gather | solution.py:28
  519.9 0.0 copy-done
  519.9 1.4 fusion.10
  521.3 0.0 all-gather.8.cloned.1.call-update
  521.3 73.8 %all-gather.8.cloned.1.call-done = bf16[1024,2,896]{0,2,1:T(8,128)(2,1)} async-done(((bf16[128,2,896]{0,2,1:T(8,128)(2,1)}), bf16[1024,2,896]{0,2,1:T(8,128)(2,1)}) %all-gather.8.cloned.1.call-update) | async-done | bytes 3670032 | tf_op jit(solution)/shard_map/all_gather | solution.py:36
  595.1 8.5 %convert_bitcast_fusion = bf16[2,1024,896]{1,2,0:T(8,128)(2,1)} fusion(bf16[1024,2,896]{0,2,1:T(8,128)(2,1)} %all-gather.8.cloned.1.call-done, bf16[1024,1024]{0,1:T(8,128)(2,1)} %all-gather.4.cloned.1.call-done), kind=kOutput, calls=%fused_computation.1 | convolution fusion | flops 3759931392 | bytes 9437184 | tf_op jit(solution)/shard_map/da,aqf->qdf/dot_general | solution.py:33
  603.7 6.0 copy.8
Async XLA Ops:
  6.5 71.6 %all-gather.4.cloned.1.call-start = ((), (), s32[]{:S(2)}) async-start(), calls=%async_computation | async-start | bytes 2162688 | tf_op jit(solution)/shard_map/all_gather | solution.py:8
  7.3 188.8 %all-reduce.5.cloned.1.call-start = ((), (), s32[]{:S(2)}) async-start(), calls=%async_computation.3 | async-start | bytes 7340032
  90.4 0.8 copy-start.4
  90.4 166.8 %all-gather.6.cloned.1.call-start = ((), (), s32[]{:S(2)}) async-start(), calls=%async_computation.1 | async-start | bytes 2064384 | tf_op jit(solution)/shard_map/all_gather | solution.py:9
  91.1 395.3 %all-reduce.7.cloned.1.call-start = ((), (), s32[]{:S(2)}) async-start(), calls=%async_computation.4 | async-start | bytes 2097152
  92.4 168.5 %copy-start.3 = (u32[256]{0:T(256)S(1)}, u32[256]{0:T(256)}, u32[]{:S(2)}) copy-start(u32[256]{0:T(256)} %constant.6) | copy-start | bytes 3076
  92.4 170.3 %copy-start.1 = (f32[128]{0:T(128)S(1)}, f32[128]{0:T(128)}, u32[]{:S(2)}) copy-start(f32[128]{0:T(128)} %param.9) | copy-start | bytes 1540
  92.4 170.3 %copy-start.2 = (f32[32]{0:T(128)S(1)}, f32[32]{0:T(128)}, u32[]{:S(2)}) copy-start(f32[32]{0:T(128)} %param.10) | copy-start | bytes 388
  257.2 262.7 %copy-start = (bf16[896,1024]{1,0:T(8,128)(2,1)S(1)}, bf16[896,1024]{1,0:T(8,128)(2,1)}, u32[]{:S(2)}) copy-start(bf16[896,1024]{1,0:T(8,128)(2,1)} %all-gather.6.cloned.1.call-done) | copy-start | bytes 5505028
  260.9 334.3 %all-gather.8.cloned.1.call-start = ((), (), s32[]{:S(2)}) async-start(), calls=%async_computation.2 | async-start | bytes 4128768 | tf_op jit(solution)/shard_map/all_gather | solution.py:36
Sparse Core Ops, SparseCore 0:
  9.2 68.8 all-gather.3
  90.5 105.5 all-reduce.4
  198.6 58.5 all-gather.5
  261.0 225.4 all-reduce.6
  521.4 73.6 all-gather.7
where the time goes:
time: 617 us; the launch traced here: 616 us
  waiting for transfers between devices  533 us (86%)
  blocking collectives  32.7 us (5%)
  matrix products  18.9 us (3%)
  local copies, waits for them, and re-layouts  15.5 us (3%)
  between operations  15.1 us (2%)
    unnamed x7, waiting for transfers between devices  329 us
    all_gather x1, waiting for transfers between devices, body(): lax.all_gather(back_half, 'row', axis=0, tiled=True)  73.8 us
    all_gather x1, waiting for transfers between devices, body(): in_rows = lax.all_gather(basis_in, 'col', axis=1, tiled=True)  70.8 us
    all_gather x1, waiting for transfers between devices, body(): out_rows = lax.all_gather(basis_out, 'row', axis=1, tiled=True)  59.8 us
    all_gather x1, blocking collectives, body(): scaled_all = lax.all_gather(scaled, 'col', axis=0, tiled=True)  32.7 us
  transfers between devices with their start and end apart: 5, of which 5 were waited for; matrix products, arithmetic and copies ran while one was open for 0% of the time, Pallas kernels for 0%

commit v1 on v0

v1 whole, which is shorter than its diff:
```python
import functools

import jax
import jax.numpy as jnp
from jax import lax
from jax.experimental import pallas as pl
from jax.experimental.pallas import tpu as pltpu
from jax.sharding import PartitionSpec as P

MESH = pl.DeviceIdType.MESH
BF = jnp.bfloat16
F32 = jnp.float32
NSEM = 160


def nt(a, b):
    return lax.dot_general(a, b, (((1,), (1,)), ((), ())), preferred_element_type=F32)


def nn(a, b):
    return lax.dot_general(a, b, (((1,), (0,)), ((), ())), preferred_element_type=F32)


def kernel(
    g_hbm, bi_in, bo_in, ei, eo, damp, out_hbm,
    g, bit, bot, yt, sibs, sibr, own, c1a, c1b, r1a, r1b, c2a, c2b, r2a, r2b, e, re, sc,
    st0, st1, bi0, bi1, acc, ob, ssem, rsem, lsem,
):
    r = lax.axis_index("row")
    c = lax.axis_index("col")
    xh, y, z, xl, k = r // 4, r % 4, c // 4, (c // 2) % 2, c % 2
    x = 2 * xh + xl

    def dev(x_, y_, z_, k_):
        return ((x_ // 2) * 4 + y_, z_ * 4 + (x_ % 2) * 2 + k_)

    xs = [(x + d) % 4 for d in (1, 2, 3)]
    ys = [(y + d) % 4 for d in (1, 2, 3)]
    zs = [(z + d) % 8 for d in range(1, 8)]
    xdev = [dev(v, y, z, k) for v in xs]
    ydev = [dev(x, v, z, k) for v in ys]
    zdev = [dev(x, y, v, k) for v in zs]
    sib = dev(x, y, z, 1 - k)
    xlp = dev(2 * xh + 1 - xl, y, z, k)
    xhp = xdev[1]

    sends = []
    counter = [0]

    def send(src, dst, to):
        i = counter[0]
        counter[0] += 1
        cp = pltpu.make_async_remote_copy(
            src_ref=src, dst_ref=dst, send_sem=ssem.at[i], recv_sem=rsem.at[i],
            device_id=to, device_id_type=MESH,
        )
        cp.start()
        sends.append(cp)
        return cp

    gcopy = pltpu.make_async_copy(g_hbm, g, lsem.at[0])
    gcopy.start()
    obo = [pltpu.make_async_copy(bo_in.at[i], bot.at[i, r], lsem.at[1 + i]) for i in range(2)]
    obi = pltpu.make_async_copy(bi_in, bit.at[z, xl, k], lsem.at[3])
    for cp in obo + [obi]:
        cp.start()

    barrier = pltpu.get_barrier_semaphore()
    partners = xdev + ydev + zdev + [sib]
    for p in partners:
        pl.semaphore_signal(barrier, inc=1, device_id=p, device_id_type=MESH)
    pl.semaphore_wait(barrier, len(partners))

    a_x = send(bo_in.at[0], bot.at[0, r], xhp)
    bi_ring = {}
    zr, zl = zdev[0], zdev[6]
    bi_ring[0, 0, 1] = send(bi_in, bit.at[z, xl, k], zr)
    bi_ring[1, 0, 1] = send(bi_in, bit.at[z, xl, k], zl)
    bi_x = send(bi_in, bit.at[z, xl, k], xlp)
    b_y = [send(bo_in.at[1], bot.at[1, r], p) for p in ydev]
    b_x0 = send(bo_in.at[1], bot.at[1, r], xhp)
    a_y = [send(bo_in.at[0], bot.at[0, r], p) for p in ydev]
    bi_sib = [send(bi_in, bit.at[z, xl, k], sib)]

    def xside(v):
        return (1 - xh) * 4 + v

    bi_x.wait_recv()
    blk = bit.at[z, 1 - xl, k]
    bi_ring[0, 1, 1] = send(blk, blk, zr)
    bi_ring[1, 1, 1] = send(blk, blk, zl)
    bi_sib.append(send(blk, blk, sib))
    a_x.wait_recv()
    blk = bot.at[0, xside(y)]
    a_xy = [send(blk, blk, p) for p in ydev]

    def ring_step(t):
        for b in range(2):
            for d in range(2):
                if (d, b, t) not in bi_ring:
                    continue
                bi_ring[d, b, t].wait_recv()
                zz = (z - t + 8) % 8 if d == 0 else (z + t) % 8
                xx = xl if b == 0 else 1 - xl
                blk = bit.at[zz, xx, k]
                if t < 3 or (t == 3 and b == d):
                    bi_ring[d, b, t + 1] = send(blk, blk, zr if d == 0 else zl)
                bi_sib.append(send(blk, blk, sib))

    ring_step(1)
    b_xy = []
    for i in (0, 2, 1):
        b_y[i].wait_recv()
        blk = bot.at[1, xh * 4 + (y + 3 - i) % 4]
        b_xy.append(send(blk, blk, xhp))
    for cp in obo + [obi, gcopy]:
        cp.wait()
    for cp in a_y:
        cp.wait_recv()
    ring_step(2)

    def y_dot(kk, h):
        lhs = bot[kk, pl.ds(4 * h, 4)].reshape(256, 896)
        for q in range(2):
            for n in range(2):
                yt[kk, h, q, :, pl.ds(512 * n, 512)] = nt(lhs, g[q, pl.ds(512 * n, 512), :]).astype(BF)

    y_dot(0, xh)
    ring_step(3)
    y_dot(1, xh)
    b_x0.wait_recv()
    for cp in b_xy:
        cp.wait_recv()
    for cp in a_xy:
        cp.wait_recv()
    ring_step(4)
    y_dot(0, 1 - xh)
    y_dot(1, 1 - xh)
    for cp in bi_sib:
        cp.wait_recv()

    chunks = [(0, 0), (1, 0), (0, 1), (1, 1)]

    def bit_cols(n):
        return bit[pl.ds(2 * n, 2)].reshape(256, 1024)

    def partial(i):
        q, h = chunks[i]
        lhs = yt[1 - k, h, q]
        for n in range(4):
            sibs[i, :, pl.ds(256 * n, 256)] = nt(lhs, bit_cols(n)).astype(BF)
        cp = send(sibs.at[i], sibr.at[i], sib)
        lhs = yt[k, h, q]
        for n in range(4):
            own[i, :, pl.ds(256 * n, 256)] = nt(lhs, bit_cols(n))
        return cp

    def first(i, cp):
        q, h = chunks[i]
        cp.wait_recv()
        for zz in range(4):
            for xx in range(2):
                rows = pl.ds(64 * zz + 32 * xx, 32)
                v = (own[i, rows, :] + sibr[i, rows, :].astype(F32)).astype(BF)
                if q == 0:
                    for hh in range(2):
                        c1a[h, 2 * hh + xx, pl.ds(32 * zz, 32), :] = v[:, 512 * hh : 512 * hh + 512]
                else:
                    for hh in range(2):
                        for yy in range(4):
                            lo = 512 * hh + 128 * yy
                            c1b[h, yy, pl.ds(128 * (2 * hh + xx) + 32 * zz, 32), :] = v[:, lo : lo + 128]
        if q == 0:
            return [send(c1a.at[h, xs[d]], r1a.at[h, d], xdev[d]) for d in (1, 0, 2)]
        return [send(c1b.at[h, ys[d]], r1b.at[h, d], ydev[d]) for d in (1, 0, 2)]

    def second(i, cps):
        q, h = chunks[i]
        for cp in cps:
            cp.wait_recv()
        if q == 0:
            for zz in range(4):
                rows = pl.ds(32 * zz, 32)
                v = c1a[h, x, rows, :].astype(F32)
                for d in range(3):
                    v = v + r1a[h, d, rows, :].astype(F32)
                v = v.astype(BF)
                for yy in range(4):
                    c2a[h, yy, rows, :] = v[:, 128 * yy : 128 * yy + 128]
            return [send(c2a.at[h, ys[d]], r2a.at[h, d], ydev[d]) for d in (1, 0, 2)]
        for xx in range(4):
            rows = pl.ds(128 * xx, 128)
            v = c1b[h, y, rows, :].astype(F32)
            for d in range(3):
                v = v + r1b[h, d, rows, :].astype(F32)
            c2b[h, xx] = v.astype(BF)
        return [send(c2b.at[h, xs[d]], r2b.at[h, d], xdev[d]) for d in (1, 0, 2)]

    def third(i, cps):
        q, h = chunks[i]
        for cp in cps:
            cp.wait_recv()
        if q == 0:
            v = c2a[h, y].astype(F32)
            for d in range(3):
                v = v + r2a[h, d].astype(F32)
        else:
            v = c2b[h, x].astype(F32)
            for d in range(3):
                v = v + r2b[h, d].astype(F32)
        v = v.astype(BF)
        for zz in range(4):
            e[4 * h + zz, q] = v[32 * zz : 32 * zz + 32, :]

    p0 = partial(0)
    p1 = partial(1)
    f0 = first(0, p0)
    p2 = partial(2)
    f1 = first(1, p1)
    p3 = partial(3)
    f2 = first(2, p2)
    f3 = first(3, p3)

    eye = (
        lax.broadcasted_iota(jnp.int32, (256, 256), 0) == lax.broadcasted_iota(jnp.int32, (256, 256), 1)
    ).astype(F32).astype(BF)
    for i in range(4):
        for n in range(4):
            v = nt(eye, bit[pl.ds(2 * n, 2), :, :, :, pl.ds(256 * i, 256)].reshape(256, 256)).astype(BF)
            rows = pl.ds(256 * i, 256)
            bi0[n // 2, rows, pl.ds(256 * (n % 2), 256)] = v
            for b in range(2):
                rr = 2 * n + b
                bi1[rr % 4, rows, pl.ds(128 * (rr // 4), 128)] = v[:, 128 * b : 128 * b + 128]

    s0 = second(0, f0)
    s1 = second(1, f1)
    s2 = second(2, f2)
    s3 = second(3, f3)
    third(0, s0)
    third(1, s1)
    third(2, s2)
    third(3, s3)
    zsend = [send(e.at[zs[d]], re.at[d], zdev[d]) for d in (3, 2, 4, 1, 5, 0, 6)]
    denom = eo[...] * ei[...] + damp[0]
    v = e[z].astype(F32)
    for cp in zsend:
        cp.wait_recv()
    for d in range(7):
        v = v + re[d].astype(F32)
    sc[...] = (v / denom[None]).astype(BF)

    yl = pl.ds(pl.multiple_of(128 * y, 128), 128)
    hl = pl.ds(pl.multiple_of(128 * xh, 128), 128)
    g0 = [send(sc.at[0], st0.at[xh, k, z, xl, :, yl], zdev[d]) for d in (3, 2, 4, 1, 5, 0, 6)]
    g1 = [send(sc.at[1], st1.at[y, k, z, xl, :, hl], zdev[d]) for d in (3, 2, 4, 1, 5, 0, 6)]
    st0[xh, k, z, xl, :, yl] = sc[0]
    st1[y, k, z, xl, :, hl] = sc[1]
    for cp in g0:
        cp.wait_recv()
    blk = st0.at[xh, k, :, xl, :, yl]
    g0 = [send(blk, blk, ydev[d]) for d in (1, 0, 2)]
    for cp in g1:
        cp.wait_recv()
    blk = st1.at[y, k, :, xl, :, hl]
    g1 = [send(blk, blk, xdev[d]) for d in (1, 0, 2)]

    def reg(q, h, v, kk):
        if q == 0:
            return st0.at[v // 2, kk, pl.ds(4 * h, 4), v % 2]
        return st1.at[v, kk, pl.ds(4 * h, 4)]

    heavy = {}
    cores = {}
    for cp in g0:
        cp.wait_recv()
    for h in range(2):
        blk = reg(0, h, x, k)
        heavy[0, h] = [send(blk, blk, xdev[d]) for d in (1, 0, 2)]
    for cp in g1:
        cp.wait_recv()
    for h in range(2):
        blk = reg(1, h, y, k)
        heavy[1, h] = [send(blk, blk, ydev[d]) for d in (1, 0, 2)]
    for h in range(2):
        for q in range(2):
            blk = reg(q, h, x if q == 0 else y, k)
            cores[q, h] = [send(blk, blk, sib)]

    def spread(q, h):
        at = x if q == 0 else y
        for i, d in enumerate((1, 0, 2)):
            heavy[q, h][i].wait_recv()
            blk = reg(q, h, (at + 3 - d) % 4, k)
            cores[q, h].append(send(blk, blk, sib))

    outs = []

    def finish(q, h):
        for cp in cores[q, h]:
            cp.wait_recv()

        def step(m):
            rows = pl.ds(pl.multiple_of(256 * m, 256), 256)
            o = None
            for kk in range(2):
                if q == 0:
                    v = nt(bi0[0, rows, :], st0[0, kk, pl.ds(4 * h, 4)].reshape(256, 512))
                    v = v + nt(bi0[1, rows, :], st0[1, kk, pl.ds(4 * h, 4)].reshape(256, 512))
                else:
                    v = nt(bi1[0, rows, :], st1[0, kk, pl.ds(4 * h, 4)].reshape(256, 256))
                    for n in range(1, 4):
                        v = v + nt(bi1[n, rows, :], st1[n, kk, pl.ds(4 * h, 4)].reshape(256, 256))
                t = nn(v.astype(BF), bot[kk, pl.ds(4 * h, 4)].reshape(256, 896))
                o = t if o is None else o + t
            if h == 0:
                acc[q, rows, :] = o
            else:
                ob[q, rows, :] = (acc[q, rows, :] + o).astype(BF)

        pl.loop(0, 4)(step)
        if h == 1:
            cp = pltpu.make_async_copy(ob.at[q], out_hbm.at[q], lsem.at[4 + q])
            cp.start()
            outs.append(cp)

    spread(0, 0)
    spread(1, 0)
    finish(0, 0)
    finish(1, 0)
    spread(0, 1)
    spread(1, 1)
    finish(0, 1)
    finish(1, 1)
    for cp in sends:
        cp.wait_send()
    for cp in outs:
        cp.wait()
    assert counter[0] <= NSEM, counter[0]


def body(query_grads, basis_in, basis_out, eig_in, eig_out, damping):
    bi = basis_in.T
    bo = basis_out.T.reshape(2, 2, 32, 896).transpose(1, 0, 2, 3).reshape(2, 64, 896)
    vm = pl.BlockSpec(memory_space=pltpu.VMEM)
    hbm = pl.BlockSpec(memory_space=pl.ANY)
    return pl.pallas_call(
        kernel,
        out_shape=jax.ShapeDtypeStruct((2, 1024, 896), BF),
        in_specs=[hbm, vm, vm, vm, vm, pl.BlockSpec(memory_space=pltpu.SMEM)],
        out_specs=hbm,
        scratch_shapes=[
            pltpu.VMEM((2, 1024, 896), BF),
            pltpu.VMEM((8, 2, 2, 32, 1024), BF),
            pltpu.VMEM((2, 8, 64, 896), BF),
            pltpu.VMEM((2, 2, 2, 256, 1024), BF),
            pltpu.VMEM((4, 256, 1024), BF),
            pltpu.VMEM((4, 256, 1024), BF),
            pltpu.VMEM((4, 256, 1024), F32),
            pltpu.VMEM((2, 4, 128, 512), BF),
            pltpu.VMEM((2, 4, 512, 128), BF),
            pltpu.VMEM((2, 3, 128, 512), BF),
            pltpu.VMEM((2, 3, 512, 128), BF),
            pltpu.VMEM((2, 4, 128, 128), BF),
            pltpu.VMEM((2, 4, 128, 128), BF),
            pltpu.VMEM((2, 3, 128, 128), BF),
            pltpu.VMEM((2, 3, 128, 128), BF),
            pltpu.VMEM((8, 2, 32, 128), BF),
            pltpu.VMEM((7, 2, 32, 128), BF),
            pltpu.VMEM((2, 32, 128), BF),
            pltpu.VMEM((2, 2, 8, 2, 32, 512), BF),
            pltpu.VMEM((4, 2, 8, 2, 32, 256), BF),
            pltpu.VMEM((2, 1024, 512), BF),
            pltpu.VMEM((4, 1024, 256), BF),
            pltpu.VMEM((2, 1024, 896), F32),
            pltpu.VMEM((2, 1024, 896), BF),
            pltpu.SemaphoreType.DMA((NSEM,)),
            pltpu.SemaphoreType.DMA((NSEM,)),
            pltpu.SemaphoreType.DMA((6,)),
        ],
        compiler_params=pltpu.CompilerParams(
            collective_id=1, has_side_effects=True, vmem_limit_bytes=60 * 1024 * 1024
        ),
        cost_estimate=pl.CostEstimate(flops=17_000_000_000, bytes_accessed=8_000_000, transcendentals=0),
    )(query_grads, bi, bo, eig_in.reshape(1, 128), eig_out.reshape(32, 1), damping)


def solution(mesh):
    return jax.shard_map(
        body,
        mesh=mesh,
        in_specs=(P(None, "row", "col"), P("row", "col"), P("col", "row"), P("row"), P("col"), P()),
        out_specs=P(None, "row", "col"),
        check_vma=False,
    )
```

time: 617 us -> 109 us (0.18)
  waiting for transfers between devices: 533 us -> 0 us
  Pallas kernels: 0 us -> 100 us
  blocking collectives: 32.7 us -> 0 us
  matrix products: 18.9 us -> 0 us
  between operations: 15.1 us -> 0.66 us
  local copies, waits for them, and re-layouts: 15.5 us -> 7.3 us
    unnamed x7 -> x0, waiting for transfers between devices: 329 us -> none
    all_gather x3 -> x0, waiting for transfers between devices: 204 us -> none  [the longest x1 73.8 us: body(): lax.all_gather(back_half, 'row', axis=0, tiled=True)]
    pallas_call x0 -> x1, Pallas kernels: none -> 100 us  [body(): pl.pallas_call(kernel, out_shape=jax.ShapeDtypeStruct((2, 1024, 896), BF)...]
    all_gather x1 -> x0, blocking collectives: 32.7 us -> none  [body(): scaled_all = lax.all_gather(scaled, 'col', axis=0, tiled=True)]
    dot_general x4 -> x0, matrix products: 18.9 us -> none  [the longest x1 8.53 us: body(): jnp.einsum('da,aqf->qdf', block, lax.all_gather(back_half, 'row', axis=0,...]
    dot_general x2 -> x0, local copies, waits for them, and re-layouts: 6.9 us -> none  [the longest x1 5.61 us: body(): jnp.einsum('qdf,da->aqf', query_grads, block, preferred_element_type=jnp....]
  transfers between devices with their start and end apart: 5 -> 0, of which waited for: 5 -> 0; matrix products, arithmetic and copies ran while one was open for 0% -> 0% of each run, Pallas kernels for 0% -> 0%
where the time goes in v1:
time: 109 us; the launch traced here: 108 us
  Pallas kernels  100 us (92%)
  local copies, waits for them, and re-layouts  7.3 us (7%)
    pallas_call x1, Pallas kernels, body(): pl.pallas_call(kernel, out_shape=jax.ShapeDtypeStruct((2, 1024, 896), BF)...  100 us
    unnamed x2, local copies, waits for them, and re-layouts  5.26 us

profile of v1, /device:TPU:1, one launch (start us, length us, event | category | flops | bytes accessed | tf_op | source)
XLA Modules:
  0.0 108.4 jit_solution(8288083200864817621)
XLA Ops:
  0.7 1.3 %copy.11.eo = f32[32,1]{1,0:T(8,128)} copy(f32[32,1]{0,1:T(1,128)} %bitcast.11) | data formatting | bytes 256 | tf_op jit(solution)/shard_map/reshape | solution.py:385
  2.0 1.1 %copy.9 = bf16[896,128]{0,1:T(8,128)(2,1)S(1)} copy(bf16[896,128]{1,0:T(8,128)(2,1)} %param.8) | data formatting | bytes 458752 | tf_op args[2]
  3.1 0.7 copy.10
  3.8 100.4 %shard_map.64 = bf16[2,1024,896]{2,1,0:T(8,128)(2,1)} custom-call(bf16[2,1024,896]{2,1,0:T(8,128)(2,1)} %g_hbm.1, bf16[32,1024]{1,0:T(8,128)(2,1)} %bitcast.12, bf16[2,64,896]{2,1,0:T(8,128)(2,1)} %bitcast.10, f32[1,128]{1,0:T(1,128)} %bitcast.13, f32[32,1]{1,0:T(8,128)} %copy.11.eo, f32[1]{0:T(128)S(6)} %copy.13.damp), custom_call_target="tpu_custom_call" | custom-call | flops 16999999488 | bytes 8000000 | tf_op jit(solution)/shard_map/pallas_call | solution.py:347
  104.2 4.2 %copy.14 = bf16[2,1024,896]{2,1,0:T(8,128)(2,1)} copy(bf16[2,1024,896]{2,1,0:T(8,128)(2,1)} %shard_map.64) | data formatting | bytes 7340032

commit v2 on v1

v2 whole, which is shorter than its diff:
```python
import functools

import jax
import jax.numpy as jnp
from jax import lax
from jax.experimental import pallas as pl
from jax.experimental.pallas import tpu as pltpu
from jax.sharding import PartitionSpec as P

MESH = pl.DeviceIdType.MESH
BF = jnp.bfloat16
F32 = jnp.float32
NSEM = 200
VMEM = 49152 * 1024


def nt(a, b):
    return lax.dot_general(a, b, (((1,), (1,)), ((), ())), preferred_element_type=F32)


def nn(a, b):
    return lax.dot_general(a, b, (((1,), (0,)), ((), ())), preferred_element_type=F32)


def kernel(
    g_hbm, bi_hbm, bo_hbm, ei_hbm, eo_hbm, damp_hbm, out_hbm,
    g, bov, bit, bot, yt, sibs, sibr, own, c1a, c1b, r1a, r1b, c2a, c2b, r2a, r2b, e, re, zg,
    st0, st1, bi0, bi1, acc, ob, ei, eo, damp, ssem, rsem, lsem, zsem,
):
    r = lax.axis_index("row")
    c = lax.axis_index("col")
    xh, y, z, xl, k = r // 4, r % 4, c // 4, (c // 2) % 2, c % 2
    x = 2 * xh + xl

    def dev(x_, y_, z_, k_):
        return ((x_ // 2) * 4 + y_, z_ * 4 + (x_ % 2) * 2 + k_)

    xs = [(x + d) % 4 for d in (1, 2, 3)]
    ys = [(y + d) % 4 for d in (1, 2, 3)]
    xdev = [dev(v, y, z, k) for v in xs]
    ydev = [dev(x, v, z, k) for v in ys]
    zdev = [None] + [dev(x, y, (z + d) % 8, k) for d in range(1, 8)]
    sib = dev(x, y, z, 1 - k)
    xlp = dev(2 * xh + 1 - xl, y, z, k)
    xhp = xdev[1]

    sends = []
    counter = [0]

    def send(src, dst, to):
        i = counter[0]
        counter[0] += 1
        cp = pltpu.make_async_remote_copy(
            src_ref=src, dst_ref=dst, send_sem=ssem.at[i], recv_sem=rsem.at[i],
            device_id=to, device_id_type=MESH,
        )
        cp.start()
        sends.append(cp)
        return cp

    def load(i, src, dst):
        cp = pltpu.make_async_copy(src, dst, lsem.at[i])
        cp.start()
        return cp

    barrier = pltpu.get_barrier_semaphore()
    partners = [xdev[1], xdev[0], xdev[2], ydev[0], ydev[2], zdev[1], zdev[7], sib]
    for p in partners:
        pl.semaphore_signal(barrier, inc=1, device_id=p, device_id_type=MESH)
    lbo = load(0, bo_hbm, bov)
    lbi = load(1, bi_hbm, bit.at[z, xl, k])
    later = [load(2, ei_hbm, ei), load(3, eo_hbm, eo), load(4, damp_hbm, damp)]
    lg = load(5, g_hbm, g)

    lbo.wait()
    to = lax.broadcasted_iota(jnp.int32, (128, 128), 0)
    at = (to // 32 % 2) * 64 + (to // 64) * 32 + to % 32
    perm = (at == lax.broadcasted_iota(jnp.int32, (128, 128), 1)).astype(F32).astype(BF)
    v = nt(perm, bov[...]).astype(BF)
    bot[0, r] = v[:64]
    bot[1, r] = v[64:]
    lbi.wait()
    pl.semaphore_wait(barrier, len(partners))

    yup, ydn = ydev[0], ydev[2]
    zr, zl = zdev[1], zdev[7]
    me = bit.at[z, xl, k]
    ring = {(0, 0, 1): send(me, me, zr), (1, 0, 1): send(me, me, zl)}
    bi_x = send(me, me, xlp)
    blk = bot.at[0, r]
    a_x = send(blk, blk, xhp)
    near = {}
    blk = bot.at[1, r]
    near[1, "own"] = [send(blk, blk, yup), send(blk, blk, ydn)]
    bi_sib = [send(me, me, sib)]

    def pass_y(kk, side, hh):
        for cp in near[kk, side]:
            cp.wait_recv()
        lo = bot.at[kk, 4 * hh + (y + 3) % 4, pl.ds(0, 32)]
        hi = bot.at[kk, 4 * hh + (y + 1) % 4, pl.ds(32, 32)]
        near[kk, side, 2] = [send(lo, lo, yup), send(hi, hi, ydn)]

    def ring_step(t, b):
        for d in range(2):
            if (d, b, t) not in ring:
                continue
            ring[d, b, t].wait_recv()
            zz = (z - t + 8) % 8 if d == 0 else (z + t) % 8
            blk = bit.at[zz, xl if b == 0 else 1 - xl, k]
            if t < 3 or (t == 3 and b == d):
                ring[d, b, t + 1] = send(blk, blk, zr if d == 0 else zl)
            bi_sib.append(send(blk, blk, sib))

    def y_dot(kk, h, q):
        lhs = bot[kk, pl.ds(4 * h, 4)].reshape(256, 896)
        for n in range(2):
            yt[kk, h, q, :, pl.ds(512 * n, 512)] = nt(lhs, g[q, pl.ds(512 * n, 512), :]).astype(BF)

    bi_x.wait_recv()
    blk = bit.at[z, 1 - xl, k]
    ring[0, 1, 1] = send(blk, blk, zr)
    ring[1, 1, 1] = send(blk, blk, zl)
    blk = bot.at[1, r]
    b_x = [send(blk, blk, xhp)]
    blk = bit.at[z, 1 - xl, k]
    bi_sib.append(send(blk, blk, sib))
    pass_y(1, "own", xh)
    for v in ((y + 3) % 4, (y + 1) % 4):
        blk = bot.at[1, 4 * xh + v]
        b_x.append(send(blk, blk, xhp))
    blk = bot.at[0, r]
    near[0, "own"] = [send(blk, blk, yup), send(blk, blk, ydn)]
    ring_step(1, 0)
    ring_step(1, 1)
    ring_step(2, 0)
    pass_y(0, "own", xh)
    ring_step(2, 1)
    ring_step(3, 0)
    a_x.wait_recv()
    blk = bot.at[0, 4 * (1 - xh) + y]
    near[0, "far"] = [send(blk, blk, yup), send(blk, blk, ydn)]
    for i, cp in enumerate(near[1, "own", 2]):
        cp.wait_recv()
        blk = bot.at[1, 4 * xh + (y + 2) % 4, pl.ds(32 * i, 32)]
        b_x.append(send(blk, blk, xhp))
    lg.wait()
    y_dot(1, xh, 0)
    y_dot(1, xh, 1)
    ring_step(3, 1)
    pass_y(0, "far", 1 - xh)
    ring_step(4, 0)
    for cp in near[0, "own", 2]:
        cp.wait_recv()
    y_dot(0, xh, 0)
    ring_step(4, 1)
    y_dot(0, xh, 1)
    for cp in near[0, "far", 2]:
        cp.wait_recv()
    y_dot(0, 1 - xh, 0)
    y_dot(0, 1 - xh, 1)
    for cp in b_x:
        cp.wait_recv()
    y_dot(1, 1 - xh, 0)
    y_dot(1, 1 - xh, 1)
    for cp in bi_sib:
        cp.wait_recv()

    chunks = [(0, 0), (1, 0), (0, 1), (1, 1)]

    def bit_cols(n):
        return bit[pl.ds(2 * n, 2)].reshape(256, 1024)

    def partial(i):
        q, h = chunks[i]
        lhs = yt[1 - k, h, q]
        for n in range(4):
            sibs[i, :, pl.ds(256 * n, 256)] = nt(lhs, bit_cols(n)).astype(BF)
        cp = send(sibs.at[i], sibr.at[i], sib)
        lhs = yt[k, h, q]
        for n in range(4):
            own[i, :, pl.ds(256 * n, 256)] = nt(lhs, bit_cols(n))
        return cp

    def first(i, cp):
        q, h = chunks[i]
        cp.wait_recv()
        for zz in range(4):
            for xx in range(2):
                rows = pl.ds(64 * zz + 32 * xx, 32)
                v = (own[i, rows, :] + sibr[i, rows, :].astype(F32)).astype(BF)
                if q == 0:
                    for hh in range(2):
                        c1a[h, 2 * hh + xx, pl.ds(32 * zz, 32), :] = v[:, 512 * hh : 512 * hh + 512]
                else:
                    for hh in range(2):
                        for yy in range(4):
                            lo = 512 * hh + 128 * yy
                            c1b[h, yy, pl.ds(128 * (2 * hh + xx) + 32 * zz, 32), :] = v[:, lo : lo + 128]
        return relay(i, 0)

    def relay(i, step):
        q, h = chunks[i]
        src, dst, n, at = (c1a, r1a, 64, x) if q == 0 else (c1b, r1b, 256, y)
        far, up, down = (at + 2) % 4, (at + 1) % 4, (at + 3) % 4
        pu, _, pd = xdev if q == 0 else ydev
        lo, hi = pl.ds(0, n), pl.ds(n, n)
        if step == 0:
            return [
                send(src.at[h, far, lo], dst.at[h, 0, lo], pu),
                send(src.at[h, far, hi], dst.at[h, 0, hi], pd),
                send(src.at[h, up, hi], dst.at[h, 1, hi], pu),
                send(src.at[h, down, lo], dst.at[h, 2, lo], pd),
            ]
        cps = firsts[i]
        cps[0].wait_recv()
        src[h, up, lo, :] = (src[h, up, lo, :].astype(F32) + dst[h, 0, lo, :].astype(F32)).astype(BF)
        a = send(src.at[h, up, lo], dst.at[h, 1, lo], pu)
        cps[1].wait_recv()
        src[h, down, hi, :] = (src[h, down, hi, :].astype(F32) + dst[h, 0, hi, :].astype(F32)).astype(BF)
        b = send(src.at[h, down, hi], dst.at[h, 2, hi], pd)
        return [cps[2], cps[3], a, b]

    def second(i, cps):
        q, h = chunks[i]
        for cp in cps:
            cp.wait_recv()
        if q == 0:
            for zz in range(4):
                rows = pl.ds(32 * zz, 32)
                v = c1a[h, x, rows, :].astype(F32)
                for d in range(1, 3):
                    v = v + r1a[h, d, rows, :].astype(F32)
                v = v.astype(BF)
                for yy in range(4):
                    c2a[h, yy, rows, :] = v[:, 128 * yy : 128 * yy + 128]
            return [send(c2a.at[h, ys[d]], r2a.at[h, d], ydev[d]) for d in (1, 0, 2)]
        for xx in range(4):
            rows = pl.ds(128 * xx, 128)
            v = c1b[h, y, rows, :].astype(F32)
            for d in range(1, 3):
                v = v + r1b[h, d, rows, :].astype(F32)
            c2b[h, xx] = v.astype(BF)
        return [send(c2b.at[h, xs[d]], r2b.at[h, d], xdev[d]) for d in (1, 0, 2)]

    def third(i, cps):
        q, h = chunks[i]
        for cp in cps:
            cp.wait_recv()
        if q == 0:
            v = c2a[h, y].astype(F32)
            for d in range(3):
                v = v + r2a[h, d].astype(F32)
        else:
            v = c2b[h, x].astype(F32)
            for d in range(3):
                v = v + r2b[h, d].astype(F32)
        v = v.astype(BF)
        for zz in range(4):
            e[4 * h + zz, q] = v[32 * zz : 32 * zz + 32, :]

    def sum_z(h, i):
        zt = 4 * h + i
        d = (zt - z + 8) % 8
        cp = pltpu.make_async_remote_copy(
            src_ref=e.at[zt], dst_ref=re.at[d], send_sem=zsem.at[0, zt], recv_sem=zsem.at[1, d],
            device_id=dev(x, y, zt, k), device_id_type=MESH,
        )
        return zt != z, cp

    def sum_z_start(h):
        for i in range(4):
            other, cp = sum_z(h, i)
            pl.when(other)(cp.start)

    def all_z(d):
        return pltpu.make_async_remote_copy(
            src_ref=zg.at[z], dst_ref=zg.at[z], send_sem=zsem.at[2, d], recv_sem=zsem.at[3, d],
            device_id=zdev[d], device_id_type=MESH,
        )

    def scale(h):
        @pl.when(z // 4 == h)
        def _():
            diag = lax.broadcasted_iota(jnp.int32, (32, 32), 0) == lax.broadcasted_iota(jnp.int32, (32, 32), 1)
            col = jnp.sum(jnp.where(diag, eo[...], 0.0), axis=1, keepdims=True)
            denom = col * ei[...] + damp[...]
            v = e[z].astype(F32)
            for d in range(1, 8):
                pltpu.make_async_remote_copy(
                    src_ref=e.at[z], dst_ref=re.at[d], send_sem=zsem.at[0, 0], recv_sem=zsem.at[1, d],
                    device_id=zdev[d], device_id_type=MESH,
                ).wait_recv()
            for d in range(1, 8):
                v = v + re[d].astype(F32)
            zg[z] = (v / denom[None]).astype(BF)
            for d in (4, 3, 5, 2, 6, 1, 7):
                all_z(d).start()

    yl = pl.ds(pl.multiple_of(128 * y, 128), 128)
    hl = pl.ds(pl.multiple_of(128 * xh, 128), 128)

    def middle(h):
        for i in range(4):
            zz = 4 * h + i
            d = (z - zz + 8) % 8

            @pl.when(zz != z)
            def _():
                pltpu.make_async_remote_copy(
                    src_ref=zg.at[zz], dst_ref=zg.at[zz], send_sem=zsem.at[2, d], recv_sem=zsem.at[3, d],
                    device_id=zdev[1], device_id_type=MESH,
                ).wait_recv()

        rows = pl.ds(4 * h, 4)
        cps0 = [send(zg.at[rows, 0], st0.at[xh, k, rows, xl, :, yl], ydev[d]) for d in (1, 0, 2)]
        cps1 = [send(zg.at[rows, 1], st1.at[y, k, rows, xl, :, hl], xdev[d]) for d in (1, 0, 2)]
        st0[xh, k, rows, xl, :, yl] = zg[rows, 0]
        st1[y, k, rows, xl, :, hl] = zg[rows, 1]
        return cps0, cps1

    def reg(q, h, v, half=None):
        rows = pl.ds(4 * h, 4) if half is None else pl.ds(4 * h + 2 * half, 2)
        if q == 0:
            return st0.at[v // 2, k, rows, v % 2]
        return st1.at[v, k, rows]

    heavy = {}
    cores = {}

    def wide(q, h, cps):
        for cp in cps:
            cp.wait_recv()
        blk = reg(q, h, x if q == 0 else y)
        to = xdev if q == 0 else ydev
        heavy[q, h] = [send(blk, blk, to[0]), send(blk, blk, to[2])]
        cores[q, h] = [send(blk, blk, sib)]

    def onward(q, h):
        to = xdev if q == 0 else ydev
        at = x if q == 0 else y
        got = heavy[q, h]
        heavy[q, h] = []
        for i in range(2):
            got[i].wait_recv()
            v = (at + 3) % 4 if i == 0 else (at + 1) % 4
            part = reg(q, h, v, i)
            heavy[q, h].append(send(part, part, to[2 * i]))
            blk = reg(q, h, v)
            cores[q, h].append(send(blk, blk, sib))

    def spread(q, h):
        for i in range(2):
            heavy[q, h][i].wait_recv()
            blk = reg(q, h, ((x if q == 0 else y) + 2) % 4, i)
            cores[q, h].append(send(blk, blk, sib))

    outs = []

    def finish(q, h):
        for cp in cores[q, h]:
            cp.wait_recv()
        basis = bi0 if q == 0 else bi1
        rows4 = pl.ds(4 * h, 4)
        for kk in range(2):
            if q == 0:
                s = [st0[n, kk, rows4].reshape(256, 512) for n in range(2)]
            else:
                s = [st1[n, kk, rows4].reshape(256, 256) for n in range(4)]
            s = jnp.concatenate(s, axis=1)
            for m in range(4):
                v = nt(basis[pl.ds(256 * m, 256), :], s).astype(BF)
                yt[q, h, m // 2, :, pl.ds(512 * (m % 2) + 256 * kk, 256)] = v
        for m in range(4):
            rows = pl.ds(256 * m, 256)
            v = yt[q, h, m // 2, :, pl.ds(512 * (m % 2), 512)]
            for lo, width in ((0, 256), (256, 256), (512, 256), (768, 128)):
                cols = pl.ds(lo, width)
                rhs = [bot[kk, rows4, :, cols].reshape(256, width) for kk in range(2)]
                o = nn(v, jnp.concatenate(rhs, axis=0))
                if h == 0:
                    acc[q, rows, cols] = o
                else:
                    ob[q, rows, cols] = (acc[q, rows, cols] + o).astype(BF)
            if h == 1 and m % 2 == 1:
                rows = pl.ds(512 * (m // 2), 512)
                cp = pltpu.make_async_copy(ob.at[q, rows], out_hbm.at[q, rows], lsem.at[6 + 2 * q + m // 2])
                cp.start()
                outs.append(cp)

    firsts = {}
    p0 = partial(0)
    p1 = partial(1)
    firsts[0] = first(0, p0)
    p2 = partial(2)
    firsts[1] = first(1, p1)
    p3 = partial(3)
    r0 = relay(0, 1)
    firsts[2] = first(2, p2)
    r1 = relay(1, 1)
    firsts[3] = first(3, p3)

    eye = (
        lax.broadcasted_iota(jnp.int32, (256, 256), 0) == lax.broadcasted_iota(jnp.int32, (256, 256), 1)
    ).astype(F32).astype(BF)
    for i in range(4):
        for n in range(4):
            v = nt(eye, bit[pl.ds(2 * n, 2), :, :, :, pl.ds(256 * i, 256)].reshape(256, 256)).astype(BF)
            rows = pl.ds(256 * i, 256)
            bi0[rows, pl.ds(256 * n, 256)] = v
            for b in range(2):
                rr = 2 * n + b
                bi1[rows, pl.ds(256 * (rr % 4) + 128 * (rr // 4), 128)] = v[:, 128 * b : 128 * b + 128]
    for cp in later:
        cp.wait()

    s0 = second(0, r0)
    s1 = second(1, r1)
    r2 = relay(2, 1)
    r3 = relay(3, 1)
    third(0, s0)
    third(1, s1)
    sum_z_start(0)
    s2 = second(2, r2)
    s3 = second(3, r3)
    third(2, s2)
    third(3, s3)
    sum_z_start(1)
    scale(0)
    scale(1)
    m0 = middle(0)
    wide(0, 0, m0[0])
    wide(1, 0, m0[1])
    m1 = middle(1)
    onward(0, 0)
    onward(1, 0)
    wide(0, 1, m1[0])
    wide(1, 1, m1[1])
    spread(0, 0)
    spread(1, 0)
    onward(0, 1)
    onward(1, 1)
    finish(0, 0)
    spread(0, 1)
    finish(1, 0)
    spread(1, 1)
    finish(0, 1)
    finish(1, 1)
    for cp in sends:
        cp.wait_send()
    for h in range(2):
        for i in range(4):
            other, cp = sum_z(h, i)
            pl.when(other)(cp.wait_send)
    for d in range(1, 8):
        all_z(d).wait_send()
    for cp in outs:
        cp.wait()
    assert counter[0] <= NSEM, counter[0]


def body(query_grads, basis_in, basis_out, eig_in, eig_out, damping):
    hbm = pl.BlockSpec(memory_space=pl.ANY)
    return pl.pallas_call(
        kernel,
        out_shape=jax.ShapeDtypeStruct((2, 1024, 896), BF),
        in_specs=[pl.BlockSpec(memory_space=pltpu.HBM)] * 6,
        out_specs=hbm,
        scratch_shapes=[
            pltpu.VMEM((2, 1024, 896), BF),
            pltpu.VMEM((896, 128), BF),
            pltpu.VMEM((8, 2, 2, 32, 1024), BF),
            pltpu.VMEM((2, 8, 64, 896), BF),
            pltpu.VMEM((2, 2, 2, 256, 1024), BF),
            pltpu.VMEM((4, 256, 1024), BF),
            pltpu.VMEM((4, 256, 1024), BF),
            pltpu.VMEM((4, 256, 1024), F32),
            pltpu.VMEM((2, 4, 128, 512), BF),
            pltpu.VMEM((2, 4, 512, 128), BF),
            pltpu.VMEM((2, 3, 128, 512), BF),
            pltpu.VMEM((2, 3, 512, 128), BF),
            pltpu.VMEM((2, 4, 128, 128), BF),
            pltpu.VMEM((2, 4, 128, 128), BF),
            pltpu.VMEM((2, 3, 128, 128), BF),
            pltpu.VMEM((2, 3, 128, 128), BF),
            pltpu.VMEM((8, 2, 32, 128), BF),
            pltpu.VMEM((8, 2, 32, 128), BF),
            pltpu.VMEM((8, 2, 32, 128), BF),
            pltpu.VMEM((2, 2, 8, 2, 32, 512), BF),
            pltpu.VMEM((4, 2, 8, 2, 32, 256), BF),
            pltpu.VMEM((1024, 1024), BF),
            pltpu.VMEM((1024, 1024), BF),
            pltpu.VMEM((2, 1024, 896), F32),
            pltpu.VMEM((2, 1024, 896), BF),
            pltpu.VMEM((1, 128), F32),
            pltpu.VMEM((1, 32), F32),
            pltpu.VMEM((1, 1), F32),
            pltpu.SemaphoreType.DMA((NSEM,)),
            pltpu.SemaphoreType.DMA((NSEM,)),
            pltpu.SemaphoreType.DMA((10,)),
            pltpu.SemaphoreType.DMA((4, 8)),
        ],
        compiler_params=pltpu.CompilerParams(
            collective_id=1, has_side_effects=True, vmem_limit_bytes=VMEM
        ),
        cost_estimate=pl.CostEstimate(flops=17_000_000_000, bytes_accessed=8_000_000, transcendentals=0),
    )(
        query_grads,
        *(
            pltpu.with_memory_space_constraint(v, pltpu.HBM)
            for v in (basis_in.T, basis_out, eig_in.reshape(1, 128), eig_out.reshape(1, 32))
        ),
        damping.reshape(1, 1),
    )


def solution(mesh):
    return jax.shard_map(
        body,
        mesh=mesh,
        in_specs=(P(None, "row", "col"), P("row", "col"), P("col", "row"), P("row"), P("col"), P()),
        out_specs=P(None, "row", "col"),
        check_vma=False,
    )
```

time: 109 us -> 93.3 us (0.86)
  Pallas kernels: 100 us -> 90.7 us
  local copies, waits for them, and re-layouts: 7.3 us -> 1.84 us
    pallas_call x1, Pallas kernels: 100 us -> 90.7 us  [body(): pl.pallas_call(kernel, out_shape=jax.ShapeDtypeStruct((2, 1024, 896), BF)...]
    unnamed x2 -> x1, local copies, waits for them, and re-layouts: 5.26 us -> 1.84 us
    reshape x1 -> x0, local copies, waits for them, and re-layouts: 1.33 us -> none  [body(): eig_out.reshape(32, 1)]
where the time goes in v2:
time: 93.3 us; the launch traced here: 93.2 us
  Pallas kernels  90.7 us (97%)
  local copies, waits for them, and re-layouts  1.84 us (2%)
    pallas_call x1, Pallas kernels, body(): pl.pallas_call(kernel, out_shape=jax.ShapeDtypeStruct((2, 1024, 896), BF)...  90.7 us

profile of v2, /device:TPU:1, one launch (start us, length us, event | category | flops | bytes accessed | tf_op | source)
XLA Modules:
  0.0 93.2 jit_solution(1503334703003472188)
XLA Ops:
  0.7 90.7 %shard_map.64 = bf16[2,1024,896]{2,1,0:T(8,128)(2,1)S(1)} custom-call(bf16[2,1024,896]{2,1,0:T(8,128)(2,1)} %g_hbm.1, bf16[32,1024]{1,0:T(8,128)(2,1)} %bitcast.5, bf16[896,128]{1,0:T(8,128)(2,1)} %bo_hbm.1, f32[1,128]{1,0:T(1,128)} %bitcast.6, f32[1,32]{1,0:T(1,128)} %bitcast.7, f32[1,1]{1,0:T(1,128)} %bitcast.4.damp_hbm), custom_call_target="tpu_custom_call" | custom-call | flops 16999999488 | bytes 8000000 | tf_op jit(solution)/shard_map/pallas_call | solution.py:464
  91.4 1.8 %copy.9 = bf16[2,1024,896]{2,1,0:T(8,128)(2,1)} copy(bf16[2,1024,896]{2,1,0:T(8,128)(2,1)S(1)} %shard_map.64) | data formatting | bytes 7340032

commit v3 on v2

--- a/solution.py
+++ b/solution.py
@@ -10,7 +10,7 @@
 MESH = pl.DeviceIdType.MESH
 BF = jnp.bfloat16
 F32 = jnp.float32
-NSEM = 200
+NSEM = 224
 VMEM = 49152 * 1024
 
 
@@ -132,29 +132,29 @@
     blk = bot.at[0, r]
     near[0, "own"] = [send(blk, blk, yup), send(blk, blk, ydn)]
     ring_step(1, 0)
-    ring_step(1, 1)
-    ring_step(2, 0)
-    pass_y(0, "own", xh)
-    ring_step(2, 1)
-    ring_step(3, 0)
-    a_x.wait_recv()
-    blk = bot.at[0, 4 * (1 - xh) + y]
-    near[0, "far"] = [send(blk, blk, yup), send(blk, blk, ydn)]
     for i, cp in enumerate(near[1, "own", 2]):
         cp.wait_recv()
         blk = bot.at[1, 4 * xh + (y + 2) % 4, pl.ds(32 * i, 32)]
         b_x.append(send(blk, blk, xhp))
+    a_x.wait_recv()
+    blk = bot.at[0, 4 * (1 - xh) + y]
+    near[0, "far"] = [send(blk, blk, yup), send(blk, blk, ydn)]
+    ring_step(1, 1)
+    ring_step(2, 0)
+    pass_y(0, "own", xh)
+    pass_y(0, "far", 1 - xh)
+    ring_step(2, 1)
+    ring_step(3, 0)
     lg.wait()
     y_dot(1, xh, 0)
     y_dot(1, xh, 1)
     ring_step(3, 1)
-    pass_y(0, "far", 1 - xh)
     ring_step(4, 0)
     for cp in near[0, "own", 2]:
         cp.wait_recv()
     y_dot(0, xh, 0)
+    y_dot(0, xh, 1)
     ring_step(4, 1)
-    y_dot(0, xh, 1)
     for cp in near[0, "far", 2]:
         cp.wait_recv()
     y_dot(0, 1 - xh, 0)
@@ -333,26 +333,24 @@
             cp.wait_recv()
         blk = reg(q, h, x if q == 0 else y)
         to = xdev if q == 0 else ydev
-        heavy[q, h] = [send(blk, blk, to[0]), send(blk, blk, to[2])]
+        a, b = [reg(q, h, x if q == 0 else y, i) for i in range(2)]
+        heavy[q, h] = [send(a, a, to[0]), send(b, b, to[2]), send(b, b, to[0]), send(a, a, to[2])]
         cores[q, h] = [send(blk, blk, sib)]
 
     def onward(q, h):
         to = xdev if q == 0 else ydev
         at = x if q == 0 else y
-        got = heavy[q, h]
-        heavy[q, h] = []
-        for i in range(2):
-            got[i].wait_recv()
-            v = (at + 3) % 4 if i == 0 else (at + 1) % 4
-            part = reg(q, h, v, i)
-            heavy[q, h].append(send(part, part, to[2 * i]))
-            blk = reg(q, h, v)
-            cores[q, h].append(send(blk, blk, sib))
-
-    def spread(q, h):
         for i in range(2):
             heavy[q, h][i].wait_recv()
-            blk = reg(q, h, ((x if q == 0 else y) + 2) % 4, i)
+            blk = reg(q, h, (at + 3) % 4 if i == 0 else (at + 1) % 4, i)
+            heavy[q, h].append(send(blk, blk, to[2 * i]))
+            cores[q, h].append(send(blk, blk, sib))
+
+    def spread(q, h):
+        at = x if q == 0 else y
+        for n, v, i in ((2, at + 3, 1), (3, at + 1, 0), (4, at + 2, 0), (5, at + 2, 1)):
+            heavy[q, h][n].wait_recv()
+            blk = reg(q, h, v % 4, i)
             cores[q, h].append(send(blk, blk, sib))
 
     outs = []
@@ -439,8 +437,8 @@
     spread(0, 0)
     spread(1, 0)
     onward(0, 1)
+    finish(0, 0)
     onward(1, 1)
-    finish(0, 0)
     spread(0, 1)
     finish(1, 0)
     spread(1, 1)

time: 93.3 us -> 92 us (0.986)
  Pallas kernels: 90.7 us -> 89.4 us
    pallas_call x1, Pallas kernels: 90.7 us -> 89.4 us  [body(): pl.pallas_call(kernel, out_shape=jax.ShapeDtypeStruct((2, 1024, 896), BF)...]
where the time goes in v3:
time: 92 us; the launch traced here: 91.9 us
  Pallas kernels  89.4 us (97%)
  local copies, waits for them, and re-layouts  1.84 us (2%)
    pallas_call x1, Pallas kernels, body(): pl.pallas_call(kernel, out_shape=jax.ShapeDtypeStruct((2, 1024, 896), BF)...  89.4 us

profile of v3, /device:TPU:1, one launch (start us, length us, event | category | flops | bytes accessed | tf_op | source)
XLA Modules:
  0.0 91.9 jit_solution(17791933290804344135)
XLA Ops:
  0.7 89.4 %shard_map.64 = bf16[2,1024,896]{2,1,0:T(8,128)(2,1)S(1)} custom-call(bf16[2,1024,896]{2,1,0:T(8,128)(2,1)} %g_hbm.1, bf16[32,1024]{1,0:T(8,128)(2,1)} %bitcast.5, bf16[896,128]{1,0:T(8,128)(2,1)} %bo_hbm.1, f32[1,128]{1,0:T(1,128)} %bitcast.6, f32[1,32]{1,0:T(1,128)} %bitcast.7, f32[1,1]{1,0:T(1,128)} %bitcast.4.damp_hbm), custom_call_target="tpu_custom_call" | custom-call | flops 16999999488 | bytes 8000000 | tf_op jit(solution)/shard_map/pallas_call | solution.py:462
  90.1 1.8 %copy.9 = bf16[2,1024,896]{2,1,0:T(8,128)(2,1)} copy(bf16[2,1024,896]{2,1,0:T(8,128)(2,1)S(1)} %shard_map.64) | data formatting | bytes 7340032
